TPU v7x, 128 devices: a whole 4x4x4 slice. The times are simulated.
128 devices in a mesh: replica: 8 (over y, z_hi), dp: 16 (over z_lo, x, core).
Axes of the slice: x: 4, y: 4, z: 4 (z_hi: 2, z_lo: 2; z = z_hi * 2 + z_lo), core: 2. Of those that a mesh axis runs over, the one named last changes fastest.
Arguments:
- tokens: bfloat16 [32768, 1152], P(('replica', 'dp')), may hold values from -6 to 6
- hidden: bfloat16 [32768, 4304], P(('replica', 'dp')), may hold values from -6 to 6
- w_out: bfloat16 [1152, 4304], replicated, may hold values from -0.09375 to 0.09375
- norm_gain: float32 [1152], replicated, may hold values from 0.1 to 1.9
- text_embed: bfloat16 [128, 1152], P(('replica', 'dp')), may hold values from -6 to 6
- logit_scale: float32 [1], replicated, may hold values from 4 to 16
- logit_bias: float32 [1], replicated, may hold values from -4 to -1
Outputs:
- loss: float32 [8], P('replica')
- grad_text: float32 [128, 1152], P(('replica', 'dp'))
- grad_tokens: bfloat16 [32768, 1152], P(('replica', 'dp'))
- grad_w_out: float32 [1152, 4304], P(('replica', 'dp'))
All inputs are finite; a program needn't handle non-finite values.
Results may differ from a plain program's by a relative error of at most 0.0029.
Values may be sent and summed in bfloat16 or wider, within the bound.
A program may use at most 128 MiB of HBM per device.

v0:
```python
import jax
import jax.numpy as jnp
from jax import lax
from jax.sharding import PartitionSpec as P


def from_behind(block, axis, distance):
    devices = range(lax.axis_size(axis))
    route = [((i - distance) % len(devices), i) for i in devices]
    return lax.ppermute(block, axis, route)


def on_device(tokens, hidden, w_out, norm_gain, text_embed, logit_scale, logit_bias):
    tok_rows, feat_width = tokens.shape
    samples = text_embed.shape[0]
    patches = tok_rows // samples
    group_size = samples * lax.axis_size("dp")
    temp_scale = logit_scale[0]
    shift_bias = logit_bias[0]
    highest = lax.Precision.HIGHEST
    residual = tokens.astype(jnp.float32) + lax.dot_general(
        hidden, w_out, (((1,), (1,)), ((), ())), preferred_element_type=jnp.float32
    )
    row_mean = jnp.mean(residual, axis=-1, keepdims=True)
    centred = residual - row_mean
    variance = jnp.mean(centred * centred, axis=-1, keepdims=True)
    inv_std = 1.0 / jnp.sqrt(variance + 1e-06)
    unit_rows = centred * inv_std
    normed = unit_rows * norm_gain
    pooled = jnp.mean(normed.reshape(samples, patches, feat_width), axis=1)
    pool_norm = jnp.sqrt(jnp.sum(pooled * pooled, axis=-1, keepdims=True) + 1e-06)
    image_emb = pooled / pool_norm

    def unit_of(text_rows):
        text_f32 = text_rows.astype(jnp.float32)
        text_norm = jnp.sqrt(jnp.sum(text_f32 * text_f32, axis=-1, keepdims=True) + 1e-06)
        return (text_f32 / text_norm, text_norm)

    def pair_terms(text_rows, positive):
        unit_text, text_norm = unit_of(text_rows)
        logits = temp_scale * jnp.dot(image_emb, unit_text.T, precision=highest) + shift_bias
        label_sign = jnp.where(positive, 1.0, -1.0).astype(jnp.float32)
        loss_part = -jnp.sum(jax.nn.log_sigmoid(label_sign * logits))
        logit_grad = -label_sign * jax.nn.sigmoid(-label_sign * logits) / group_size
        image_grad = temp_scale * jnp.dot(logit_grad, unit_text, precision=highest)
        unit_grad = temp_scale * jnp.dot(logit_grad.T, image_emb, precision=highest)
        return (loss_part, image_grad, unit_grad)

    diagonal_mask = jnp.eye(samples, dtype=bool)

    def travel(visit, carry):
        text_block, carried, image_total, loss_total = carry
        positive = jnp.logical_and(diagonal_mask, visit == 0)
        loss_part, image_grad, unit_grad = pair_terms(text_block, positive)
        carried = carried + unit_grad
        text_block = from_behind(text_block, "dp", 1)
        carried = from_behind(carried, "dp", 1)
        return (text_block, carried, image_total + image_grad, loss_total + loss_part)

    start_carry = (
        text_embed,
        jnp.zeros((samples, feat_width), jnp.float32),
        jnp.zeros((samples, feat_width), jnp.float32),
        jnp.zeros((), jnp.float32),
    )
    final_carry = lax.fori_loop(0, lax.axis_size("dp"), travel, start_carry)
    own_grad = final_carry[1]
    image_grad = final_carry[2]
    loss_local = final_carry[3]
    group_loss = lax.psum(loss_local, "dp") / group_size
    own_unit, own_norm = unit_of(text_embed)
    grad_text = (
        own_grad - own_unit * jnp.sum(own_unit * own_grad, axis=-1, keepdims=True)
    ) / own_norm
    pooled_grad = (
        image_grad - image_emb * jnp.sum(image_emb * image_grad, axis=-1, keepdims=True)
    ) / pool_norm
    normed_grad = jnp.broadcast_to(
        pooled_grad[:, None, :] / patches, (samples, patches, feat_width)
    ).reshape(tok_rows, feat_width)
    scaled_grad = normed_grad * norm_gain
    tok_grad = (
        scaled_grad
        - jnp.mean(scaled_grad, axis=-1, keepdims=True)
        - unit_rows * jnp.mean(scaled_grad * unit_rows, axis=-1, keepdims=True)
    ) * inv_std
    tok_grad = tok_grad.astype(jnp.bfloat16)
    grad_weight = lax.psum_scatter(
        lax.dot_general(
            tok_grad, hidden, (((0,), (0,)), ((), ())), preferred_element_type=jnp.float32
        ),
        ("replica", "dp"),
        scatter_dimension=0,
        tiled=True,
    )
    return (jnp.reshape(group_loss, (1,)), grad_text, tok_grad, grad_weight)


def solution(mesh):
    return jax.shard_map(
        on_device,
        mesh=mesh,
        in_specs=(
            P(("replica", "dp"), None),
            P(("replica", "dp"), None),
            P(),
            P(),
            P(("replica", "dp"), None),
            P(),
            P(),
        ),
        out_specs=(
            P("replica"),
            P(("replica", "dp"), None),
            P(("replica", "dp"), None),
            P(("replica", "dp"), None),
        ),
        check_vma=False,
    )
```

profile of v0, /device:TPU:1, one launch (start us, length us, event | category | flops | bytes accessed | tf_op | source)
XLA Modules:
  0.0 423.7 jit_solution(9474973280474746553)
XLA Ops:
  7.2 1.4 multiply_reduce_fusion.9
  8.8 7.1 %fusion.2 = (f32[256]{0:T(256)S(1)}, f32[256,1152]{1,0:T(8,128)S(1)}) fusion(bf16[256,4304]{0,1:T(8,128)(2,1)S(1)} %copy-done, bf16[1152,4304]{0,1:T(8,128)(2,1)} %param.11, bf16[256,1152]{1,0:T(8,128)(2,1)} %param.9), kind=kOutput, calls=%fused_computation.28 | convolution fusion | flops 2539486976 | bytes 13890560 | tf_op jit(solution)/shard_map/dot_general | solution.py:21
  18.9 155.4 %while.20 = (s32[]{:T(128)}, bf16[1,1152]{1,0:T(2,128)(2,1)S(1)}, f32[1,1152]{1,0:T(1,128)S(1)}, f32[1,1152]{1,0:T(1,128)S(1)}, f32[]{:T(128)}, /*index=5*/f32[]...) while((s32[]{:T(128)}, bf16[1,1152]{1,0:T(2,128)(2,1)S(1)}, ...), condition=%wide.region_6.7_spmd.clone, body=%wide.region_4.6_spmd.clone.sunk | while | flops 16149 | bytes 106522 | solution.py:66
  18.9 2.7 collective-permute-start
  27.5 1.9 collective-permute-start
  34.9 0.8 collective-permute-done.1
  35.7 1.4 collective-permute-start
  42.7 2.9 collective-permute-done.1
  51.2 4.3 %collective-permute-done.1 = f32[1,1152]{1,0:T(1,128)S(1)} collective-permute-done((f32[1,1152]{1,0:T(1,128)S(1)}, f32[1,1152]{1,0:T(1,128)S(1)}, u32[]{:S(2)}, u32[]{:S(2)}) %collective-permute-start.1) | collective-permute-done | bytes 4640 | tf_op jit(solution)/shard_map/while/body/eval_jaxpr/ppermute | solution.py:10
  60.3 0.7 multiply_multiply_fusion.5
  61.1 4.3 %collective-permute-done.1 = f32[1,1152]{1,0:T(1,128)S(1)} collective-permute-done((f32[1,1152]{1,0:T(1,128)S(1)}, f32[1,1152]{1,0:T(1,128)S(1)}, u32[]{:S(2)}, u32[]{:S(2)}) %collective-permute-start.1) | collective-permute-done | bytes 4640 | tf_op jit(solution)/shard_map/while/body/eval_jaxpr/ppermute | solution.py:10
  70.2 0.7 multiply_multiply_fusion.5
  71.0 4.3 %collective-permute-done.1 = f32[1,1152]{1,0:T(1,128)S(1)} collective-permute-done((f32[1,1152]{1,0:T(1,128)S(1)}, f32[1,1152]{1,0:T(1,128)S(1)}, u32[]{:S(2)}, u32[]{:S(2)}) %collective-permute-start.1) | collective-permute-done | bytes 4640 | tf_op jit(solution)/shard_map/while/body/eval_jaxpr/ppermute | solution.py:10
  80.9 4.3 %collective-permute-done.1 = f32[1,1152]{1,0:T(1,128)S(1)} collective-permute-done((f32[1,1152]{1,0:T(1,128)S(1)}, f32[1,1152]{1,0:T(1,128)S(1)}, u32[]{:S(2)}, u32[]{:S(2)}) %collective-permute-start.1) | collective-permute-done | bytes 4640 | tf_op jit(solution)/shard_map/while/body/eval_jaxpr/ppermute | solution.py:10
  90.0 0.7 multiply_multiply_fusion.5
  90.8 4.3 %collective-permute-done.1 = f32[1,1152]{1,0:T(1,128)S(1)} collective-permute-done((f32[1,1152]{1,0:T(1,128)S(1)}, f32[1,1152]{1,0:T(1,128)S(1)}, u32[]{:S(2)}, u32[]{:S(2)}) %collective-permute-start.1) | collective-permute-done | bytes 4640 | tf_op jit(solution)/shard_map/while/body/eval_jaxpr/ppermute | solution.py:10
  99.9 0.7 multiply_multiply_fusion.5
  100.7 4.3 %collective-permute-done.1 = f32[1,1152]{1,0:T(1,128)S(1)} collective-permute-done((f32[1,1152]{1,0:T(1,128)S(1)}, f32[1,1152]{1,0:T(1,128)S(1)}, u32[]{:S(2)}, u32[]{:S(2)}) %collective-permute-start.1) | collective-permute-done | bytes 4640 | tf_op jit(solution)/shard_map/while/body/eval_jaxpr/ppermute | solution.py:10
  110.6 4.3 %collective-permute-done.1 = f32[1,1152]{1,0:T(1,128)S(1)} collective-permute-done((f32[1,1152]{1,0:T(1,128)S(1)}, f32[1,1152]{1,0:T(1,128)S(1)}, u32[]{:S(2)}, u32[]{:S(2)}) %collective-permute-start.1) | collective-permute-done | bytes 4640 | tf_op jit(solution)/shard_map/while/body/eval_jaxpr/ppermute | solution.py:10
  120.5 4.3 %collective-permute-done.1 = f32[1,1152]{1,0:T(1,128)S(1)} collective-permute-done((f32[1,1152]{1,0:T(1,128)S(1)}, f32[1,1152]{1,0:T(1,128)S(1)}, u32[]{:S(2)}, u32[]{:S(2)}) %collective-permute-start.1) | collective-permute-done | bytes 4640 | tf_op jit(solution)/shard_map/while/body/eval_jaxpr/ppermute | solution.py:10
  130.4 4.3 %collective-permute-done.1 = f32[1,1152]{1,0:T(1,128)S(1)} collective-permute-done((f32[1,1152]{1,0:T(1,128)S(1)}, f32[1,1152]{1,0:T(1,128)S(1)}, u32[]{:S(2)}, u32[]{:S(2)}) %collective-permute-start.1) | collective-permute-done | bytes 4640 | tf_op jit(solution)/shard_map/while/body/eval_jaxpr/ppermute | solution.py:10
  140.3 4.3 %collective-permute-done.1 = f32[1,1152]{1,0:T(1,128)S(1)} collective-permute-done((f32[1,1152]{1,0:T(1,128)S(1)}, f32[1,1152]{1,0:T(1,128)S(1)}, u32[]{:S(2)}, u32[]{:S(2)}) %collective-permute-start.1) | collective-permute-done | bytes 4640 | tf_op jit(solution)/shard_map/while/body/eval_jaxpr/ppermute | solution.py:10
  150.2 4.3 %collective-permute-done.1 = f32[1,1152]{1,0:T(1,128)S(1)} collective-permute-done((f32[1,1152]{1,0:T(1,128)S(1)}, f32[1,1152]{1,0:T(1,128)S(1)}, u32[]{:S(2)}, u32[]{:S(2)}) %collective-permute-start.1) | collective-permute-done | bytes 4640 | tf_op jit(solution)/shard_map/while/body/eval_jaxpr/ppermute | solution.py:10
  160.1 4.3 %collective-permute-done.1 = f32[1,1152]{1,0:T(1,128)S(1)} collective-permute-done((f32[1,1152]{1,0:T(1,128)S(1)}, f32[1,1152]{1,0:T(1,128)S(1)}, u32[]{:S(2)}, u32[]{:S(2)}) %collective-permute-start.1) | collective-permute-done | bytes 4640 | tf_op jit(solution)/shard_map/while/body/eval_jaxpr/ppermute | solution.py:10
  170.0 4.3 %collective-permute-done.1 = f32[1,1152]{1,0:T(1,128)S(1)} collective-permute-done((f32[1,1152]{1,0:T(1,128)S(1)}, f32[1,1152]{1,0:T(1,128)S(1)}, u32[]{:S(2)}, u32[]{:S(2)}) %collective-permute-start.1) | collective-permute-done | bytes 4640 | tf_op jit(solution)/shard_map/while/body/eval_jaxpr/ppermute | solution.py:10
  174.9 1.3 multiply_reduce_fusion.8
  178.2 0.8 copy-done.1
  179.0 8.3 %fusion.3 = f32[1152,4304]{1,0:T(8,128)} fusion(bf16[256,1152]{1,0:T(8,128)(2,1)S(1)} %multiply_convert_fusion, bf16[256,4304]{0,1:T(8,128)(2,1)S(1)} %copy-done), kind=kOutput, calls=%fused_computation.29 | convolution fusion | flops 2538602496 | bytes 22626304 | tf_op jit(solution)/shard_map/dot_general | solution.py:89
  187.3 32.3 %psum.7 = f32[]{:T(128)} all-reduce(f32[]{:T(128)} %get-tuple-element.160), channel_id=1, replica_groups=mesh['replica'=8,'dp'=16] {'dp'}, use_global_device_ids=true, to_apply=%region_7.8 | all-reduce | flops 1 | bytes 8 | tf_op jit(solution)/shard_map/psum | solution.py:70
  220.3 1.3 subtract_divide_fusion
  221.6 192.4 %all-reduce.3.cloned.1.call-done = f32[1152,4304]{1,0:T(8,128)} async-done(((f32[1152,4304]{1,0:T(8,128)}), f32[1152,4304]{1,0:T(8,128)}) %all-reduce.3.cloned.1.call-update) | async-done | bytes 19832848
  414.0 1.7 constant_dynamic-slice_fusion
  (212 shorter events, 44.1 us)
Async XLA Ops:
  7.2 406.8 %all-reduce.3.cloned.1.call-start = ((), (), s32[]{:S(2)}) async-start(), calls=%async_computation | async-start | bytes 40108032
  18.9 8.2 %collective-permute-start = (bf16[1,1152]{1,0:T(2,128)(2,1)S(1)}, bf16[1,1152]{1,0:T(2,128)(2,1)S(1)}, u32[]{:S(2)}, u32[]{:S(2)}) collective-permute-start(bf16[1,1152]{1,0:T(2,128)(2,1)S(1)} %copy.19), channel_id=1, source_target_pairs={{15,0},{0,1},{1,2},{2,3},{3,4},{4,5},{5,6},{6,7},{7,8},{8,9},{9,10... | collective-permute-start | bytes 6920 | tf_op jit(solution)/shard_map/while/body/eval_jaxpr/ppermute | solution.py:10
  27.5 7.4 %collective-permute-start = (bf16[1,1152]{1,0:T(2,128)(2,1)S(1)}, bf16[1,1152]{1,0:T(2,128)(2,1)S(1)}, u32[]{:S(2)}, u32[]{:S(2)}) collective-permute-start(bf16[1,1152]{1,0:T(2,128)(2,1)S(1)} %copy.19), channel_id=1, source_target_pairs={{15,0},{0,1},{1,2},{2,3},{3,4},{4,5},{5,6},{6,7},{7,8},{8,9},{9,10... | collective-permute-start | bytes 6920 | tf_op jit(solution)/shard_map/while/body/eval_jaxpr/ppermute | solution.py:10
  34.1 1.7 collective-permute-start.1
  35.7 7.0 %collective-permute-start = (bf16[1,1152]{1,0:T(2,128)(2,1)S(1)}, bf16[1,1152]{1,0:T(2,128)(2,1)S(1)}, u32[]{:S(2)}, u32[]{:S(2)}) collective-permute-start(bf16[1,1152]{1,0:T(2,128)(2,1)S(1)} %copy.19), channel_id=1, source_target_pairs={{15,0},{0,1},{1,2},{2,3},{3,4},{4,5},{5,6},{6,7},{7,8},{8,9},{9,10... | collective-permute-start | bytes 6920 | tf_op jit(solution)/shard_map/while/body/eval_jaxpr/ppermute | solution.py:10
  41.9 3.8 collective-permute-start.1
  45.6 5.5 %collective-permute-start = (bf16[1,1152]{1,0:T(2,128)(2,1)S(1)}, bf16[1,1152]{1,0:T(2,128)(2,1)S(1)}, u32[]{:S(2)}, u32[]{:S(2)}) collective-permute-start(bf16[1,1152]{1,0:T(2,128)(2,1)S(1)} %copy.19), channel_id=1, source_target_pairs={{15,0},{0,1},{1,2},{2,3},{3,4},{4,5},{5,6},{6,7},{7,8},{8,9},{9,10... | collective-permute-start | bytes 6920 | tf_op jit(solution)/shard_map/while/body/eval_jaxpr/ppermute | solution.py:10
  50.3 5.2 %collective-permute-start.1 = (f32[1,1152]{1,0:T(1,128)S(1)}, f32[1,1152]{1,0:T(1,128)S(1)}, u32[]{:S(2)}, u32[]{:S(2)}) collective-permute-start(f32[1,1152]{1,0:T(1,128)S(1)} %reshape_add_fusion.2), channel_id=1, source_target_pairs={{15,0},{0,1},{1,2},{2,3},{3,4},{4,5},{5,6},{6,7},{7,8},{8,9},{9,10... | collective-permute-start | bytes 13832 | tf_op jit(solution)/shard_map/while/body/eval_jaxpr/ppermute | solution.py:10
  55.5 5.5 %collective-permute-start = (bf16[1,1152]{1,0:T(2,128)(2,1)S(1)}, bf16[1,1152]{1,0:T(2,128)(2,1)S(1)}, u32[]{:S(2)}, u32[]{:S(2)}) collective-permute-start(bf16[1,1152]{1,0:T(2,128)(2,1)S(1)} %copy.19), channel_id=1, source_target_pairs={{15,0},{0,1},{1,2},{2,3},{3,4},{4,5},{5,6},{6,7},{7,8},{8,9},{9,10... | collective-permute-start | bytes 6920 | tf_op jit(solution)/shard_map/while/body/eval_jaxpr/ppermute | solution.py:10
  60.2 5.2 %collective-permute-start.1 = (f32[1,1152]{1,0:T(1,128)S(1)}, f32[1,1152]{1,0:T(1,128)S(1)}, u32[]{:S(2)}, u32[]{:S(2)}) collective-permute-start(f32[1,1152]{1,0:T(1,128)S(1)} %reshape_add_fusion.2), channel_id=1, source_target_pairs={{15,0},{0,1},{1,2},{2,3},{3,4},{4,5},{5,6},{6,7},{7,8},{8,9},{9,10... | collective-permute-start | bytes 13832 | tf_op jit(solution)/shard_map/while/body/eval_jaxpr/ppermute | solution.py:10
  65.4 5.5 %collective-permute-start = (bf16[1,1152]{1,0:T(2,128)(2,1)S(1)}, bf16[1,1152]{1,0:T(2,128)(2,1)S(1)}, u32[]{:S(2)}, u32[]{:S(2)}) collective-permute-start(bf16[1,1152]{1,0:T(2,128)(2,1)S(1)} %copy.19), channel_id=1, source_target_pairs={{15,0},{0,1},{1,2},{2,3},{3,4},{4,5},{5,6},{6,7},{7,8},{8,9},{9,10... | collective-permute-start | bytes 6920 | tf_op jit(solution)/shard_map/while/body/eval_jaxpr/ppermute | solution.py:10
  70.1 5.2 %collective-permute-start.1 = (f32[1,1152]{1,0:T(1,128)S(1)}, f32[1,1152]{1,0:T(1,128)S(1)}, u32[]{:S(2)}, u32[]{:S(2)}) collective-permute-start(f32[1,1152]{1,0:T(1,128)S(1)} %reshape_add_fusion.2), channel_id=1, source_target_pairs={{15,0},{0,1},{1,2},{2,3},{3,4},{4,5},{5,6},{6,7},{7,8},{8,9},{9,10... | collective-permute-start | bytes 13832 | tf_op jit(solution)/shard_map/while/body/eval_jaxpr/ppermute | solution.py:10
  75.3 5.5 %collective-permute-start = (bf16[1,1152]{1,0:T(2,128)(2,1)S(1)}, bf16[1,1152]{1,0:T(2,128)(2,1)S(1)}, u32[]{:S(2)}, u32[]{:S(2)}) collective-permute-start(bf16[1,1152]{1,0:T(2,128)(2,1)S(1)} %copy.19), channel_id=1, source_target_pairs={{15,0},{0,1},{1,2},{2,3},{3,4},{4,5},{5,6},{6,7},{7,8},{8,9},{9,10... | collective-permute-start | bytes 6920 | tf_op jit(solution)/shard_map/while/body/eval_jaxpr/ppermute | solution.py:10
  80.0 5.2 %collective-permute-start.1 = (f32[1,1152]{1,0:T(1,128)S(1)}, f32[1,1152]{1,0:T(1,128)S(1)}, u32[]{:S(2)}, u32[]{:S(2)}) collective-permute-start(f32[1,1152]{1,0:T(1,128)S(1)} %reshape_add_fusion.2), channel_id=1, source_target_pairs={{15,0},{0,1},{1,2},{2,3},{3,4},{4,5},{5,6},{6,7},{7,8},{8,9},{9,10... | collective-permute-start | bytes 13832 | tf_op jit(solution)/shard_map/while/body/eval_jaxpr/ppermute | solution.py:10
  85.2 5.5 %collective-permute-start = (bf16[1,1152]{1,0:T(2,128)(2,1)S(1)}, bf16[1,1152]{1,0:T(2,128)(2,1)S(1)}, u32[]{:S(2)}, u32[]{:S(2)}) collective-permute-start(bf16[1,1152]{1,0:T(2,128)(2,1)S(1)} %copy.19), channel_id=1, source_target_pairs={{15,0},{0,1},{1,2},{2,3},{3,4},{4,5},{5,6},{6,7},{7,8},{8,9},{9,10... | collective-permute-start | bytes 6920 | tf_op jit(solution)/shard_map/while/body/eval_jaxpr/ppermute | solution.py:10
  89.9 5.2 %collective-permute-start.1 = (f32[1,1152]{1,0:T(1,128)S(1)}, f32[1,1152]{1,0:T(1,128)S(1)}, u32[]{:S(2)}, u32[]{:S(2)}) collective-permute-start(f32[1,1152]{1,0:T(1,128)S(1)} %reshape_add_fusion.2), channel_id=1, source_target_pairs={{15,0},{0,1},{1,2},{2,3},{3,4},{4,5},{5,6},{6,7},{7,8},{8,9},{9,10... | collective-permute-start | bytes 13832 | tf_op jit(solution)/shard_map/while/body/eval_jaxpr/ppermute | solution.py:10
  95.1 5.5 %collective-permute-start = (bf16[1,1152]{1,0:T(2,128)(2,1)S(1)}, bf16[1,1152]{1,0:T(2,128)(2,1)S(1)}, u32[]{:S(2)}, u32[]{:S(2)}) collective-permute-start(bf16[1,1152]{1,0:T(2,128)(2,1)S(1)} %copy.19), channel_id=1, source_target_pairs={{15,0},{0,1},{1,2},{2,3},{3,4},{4,5},{5,6},{6,7},{7,8},{8,9},{9,10... | collective-permute-start | bytes 6920 | tf_op jit(solution)/shard_map/while/body/eval_jaxpr/ppermute | solution.py:10
  99.8 5.2 %collective-permute-start.1 = (f32[1,1152]{1,0:T(1,128)S(1)}, f32[1,1152]{1,0:T(1,128)S(1)}, u32[]{:S(2)}, u32[]{:S(2)}) collective-permute-start(f32[1,1152]{1,0:T(1,128)S(1)} %reshape_add_fusion.2), channel_id=1, source_target_pairs={{15,0},{0,1},{1,2},{2,3},{3,4},{4,5},{5,6},{6,7},{7,8},{8,9},{9,10... | collective-permute-start | bytes 13832 | tf_op jit(solution)/shard_map/while/body/eval_jaxpr/ppermute | solution.py:10
  105.0 5.5 %collective-permute-start = (bf16[1,1152]{1,0:T(2,128)(2,1)S(1)}, bf16[1,1152]{1,0:T(2,128)(2,1)S(1)}, u32[]{:S(2)}, u32[]{:S(2)}) collective-permute-start(bf16[1,1152]{1,0:T(2,128)(2,1)S(1)} %copy.19), channel_id=1, source_target_pairs={{15,0},{0,1},{1,2},{2,3},{3,4},{4,5},{5,6},{6,7},{7,8},{8,9},{9,10... | collective-permute-start | bytes 6920 | tf_op jit(solution)/shard_map/while/body/eval_jaxpr/ppermute | solution.py:10
  109.7 5.2 %collective-permute-start.1 = (f32[1,1152]{1,0:T(1,128)S(1)}, f32[1,1152]{1,0:T(1,128)S(1)}, u32[]{:S(2)}, u32[]{:S(2)}) collective-permute-start(f32[1,1152]{1,0:T(1,128)S(1)} %reshape_add_fusion.2), channel_id=1, source_target_pairs={{15,0},{0,1},{1,2},{2,3},{3,4},{4,5},{5,6},{6,7},{7,8},{8,9},{9,10... | collective-permute-start | bytes 13832 | tf_op jit(solution)/shard_map/while/body/eval_jaxpr/ppermute | solution.py:10
  114.9 5.5 %collective-permute-start = (bf16[1,1152]{1,0:T(2,128)(2,1)S(1)}, bf16[1,1152]{1,0:T(2,128)(2,1)S(1)}, u32[]{:S(2)}, u32[]{:S(2)}) collective-permute-start(bf16[1,1152]{1,0:T(2,128)(2,1)S(1)} %copy.19), channel_id=1, source_target_pairs={{15,0},{0,1},{1,2},{2,3},{3,4},{4,5},{5,6},{6,7},{7,8},{8,9},{9,10... | collective-permute-start | bytes 6920 | tf_op jit(solution)/shard_map/while/body/eval_jaxpr/ppermute | solution.py:10
  119.6 5.2 %collective-permute-start.1 = (f32[1,1152]{1,0:T(1,128)S(1)}, f32[1,1152]{1,0:T(1,128)S(1)}, u32[]{:S(2)}, u32[]{:S(2)}) collective-permute-start(f32[1,1152]{1,0:T(1,128)S(1)} %reshape_add_fusion.2), channel_id=1, source_target_pairs={{15,0},{0,1},{1,2},{2,3},{3,4},{4,5},{5,6},{6,7},{7,8},{8,9},{9,10... | collective-permute-start | bytes 13832 | tf_op jit(solution)/shard_map/while/body/eval_jaxpr/ppermute | solution.py:10
  124.8 5.5 %collective-permute-start = (bf16[1,1152]{1,0:T(2,128)(2,1)S(1)}, bf16[1,1152]{1,0:T(2,128)(2,1)S(1)}, u32[]{:S(2)}, u32[]{:S(2)}) collective-permute-start(bf16[1,1152]{1,0:T(2,128)(2,1)S(1)} %copy.19), channel_id=1, source_target_pairs={{15,0},{0,1},{1,2},{2,3},{3,4},{4,5},{5,6},{6,7},{7,8},{8,9},{9,10... | collective-permute-start | bytes 6920 | tf_op jit(solution)/shard_map/while/body/eval_jaxpr/ppermute | solution.py:10
  129.5 5.2 %collective-permute-start.1 = (f32[1,1152]{1,0:T(1,128)S(1)}, f32[1,1152]{1,0:T(1,128)S(1)}, u32[]{:S(2)}, u32[]{:S(2)}) collective-permute-start(f32[1,1152]{1,0:T(1,128)S(1)} %reshape_add_fusion.2), channel_id=1, source_target_pairs={{15,0},{0,1},{1,2},{2,3},{3,4},{4,5},{5,6},{6,7},{7,8},{8,9},{9,10... | collective-permute-start | bytes 13832 | tf_op jit(solution)/shard_map/while/body/eval_jaxpr/ppermute | solution.py:10
  134.7 5.5 %collective-permute-start = (bf16[1,1152]{1,0:T(2,128)(2,1)S(1)}, bf16[1,1152]{1,0:T(2,128)(2,1)S(1)}, u32[]{:S(2)}, u32[]{:S(2)}) collective-permute-start(bf16[1,1152]{1,0:T(2,128)(2,1)S(1)} %copy.19), channel_id=1, source_target_pairs={{15,0},{0,1},{1,2},{2,3},{3,4},{4,5},{5,6},{6,7},{7,8},{8,9},{9,10... | collective-permute-start | bytes 6920 | tf_op jit(solution)/shard_map/while/body/eval_jaxpr/ppermute | solution.py:10
  139.4 5.2 %collective-permute-start.1 = (f32[1,1152]{1,0:T(1,128)S(1)}, f32[1,1152]{1,0:T(1,128)S(1)}, u32[]{:S(2)}, u32[]{:S(2)}) collective-permute-start(f32[1,1152]{1,0:T(1,128)S(1)} %reshape_add_fusion.2), channel_id=1, source_target_pairs={{15,0},{0,1},{1,2},{2,3},{3,4},{4,5},{5,6},{6,7},{7,8},{8,9},{9,10... | collective-permute-start | bytes 13832 | tf_op jit(solution)/shard_map/while/body/eval_jaxpr/ppermute | solution.py:10
  144.6 5.5 %collective-permute-start = (bf16[1,1152]{1,0:T(2,128)(2,1)S(1)}, bf16[1,1152]{1,0:T(2,128)(2,1)S(1)}, u32[]{:S(2)}, u32[]{:S(2)}) collective-permute-start(bf16[1,1152]{1,0:T(2,128)(2,1)S(1)} %copy.19), channel_id=1, source_target_pairs={{15,0},{0,1},{1,2},{2,3},{3,4},{4,5},{5,6},{6,7},{7,8},{8,9},{9,10... | collective-permute-start | bytes 6920 | tf_op jit(solution)/shard_map/while/body/eval_jaxpr/ppermute | solution.py:10
  149.3 5.2 %collective-permute-start.1 = (f32[1,1152]{1,0:T(1,128)S(1)}, f32[1,1152]{1,0:T(1,128)S(1)}, u32[]{:S(2)}, u32[]{:S(2)}) collective-permute-start(f32[1,1152]{1,0:T(1,128)S(1)} %reshape_add_fusion.2), channel_id=1, source_target_pairs={{15,0},{0,1},{1,2},{2,3},{3,4},{4,5},{5,6},{6,7},{7,8},{8,9},{9,10... | collective-permute-start | bytes 13832 | tf_op jit(solution)/shard_map/while/body/eval_jaxpr/ppermute | solution.py:10
  154.5 5.5 %collective-permute-start = (bf16[1,1152]{1,0:T(2,128)(2,1)S(1)}, bf16[1,1152]{1,0:T(2,128)(2,1)S(1)}, u32[]{:S(2)}, u32[]{:S(2)}) collective-permute-start(bf16[1,1152]{1,0:T(2,128)(2,1)S(1)} %copy.19), channel_id=1, source_target_pairs={{15,0},{0,1},{1,2},{2,3},{3,4},{4,5},{5,6},{6,7},{7,8},{8,9},{9,10... | collective-permute-start | bytes 6920 | tf_op jit(solution)/shard_map/while/body/eval_jaxpr/ppermute | solution.py:10
  159.2 5.2 %collective-permute-start.1 = (f32[1,1152]{1,0:T(1,128)S(1)}, f32[1,1152]{1,0:T(1,128)S(1)}, u32[]{:S(2)}, u32[]{:S(2)}) collective-permute-start(f32[1,1152]{1,0:T(1,128)S(1)} %reshape_add_fusion.2), channel_id=1, source_target_pairs={{15,0},{0,1},{1,2},{2,3},{3,4},{4,5},{5,6},{6,7},{7,8},{8,9},{9,10... | collective-permute-start | bytes 13832 | tf_op jit(solution)/shard_map/while/body/eval_jaxpr/ppermute | solution.py:10
  164.4 5.5 %collective-permute-start = (bf16[1,1152]{1,0:T(2,128)(2,1)S(1)}, bf16[1,1152]{1,0:T(2,128)(2,1)S(1)}, u32[]{:S(2)}, u32[]{:S(2)}) collective-permute-start(bf16[1,1152]{1,0:T(2,128)(2,1)S(1)} %copy.19), channel_id=1, source_target_pairs={{15,0},{0,1},{1,2},{2,3},{3,4},{4,5},{5,6},{6,7},{7,8},{8,9},{9,10... | collective-permute-start | bytes 6920 | tf_op jit(solution)/shard_map/while/body/eval_jaxpr/ppermute | solution.py:10
  169.1 5.2 %collective-permute-start.1 = (f32[1,1152]{1,0:T(1,128)S(1)}, f32[1,1152]{1,0:T(1,128)S(1)}, u32[]{:S(2)}, u32[]{:S(2)}) collective-permute-start(f32[1,1152]{1,0:T(1,128)S(1)} %reshape_add_fusion.2), channel_id=1, source_target_pairs={{15,0},{0,1},{1,2},{2,3},{3,4},{4,5},{5,6},{6,7},{7,8},{8,9},{9,10... | collective-permute-start | bytes 13832 | tf_op jit(solution)/shard_map/while/body/eval_jaxpr/ppermute | solution.py:10
  (6 other events, 165.7 us)
Sparse Core Ops, SparseCore 0:
  187.5 226.4 all-reduce.2
where the time goes:
time: 425 us; the launch traced here: 424 us
  waiting for transfers between devices  253 us (60%)
  other arithmetic  48.3 us (11%)
  loops' own time  46.2 us (11%)
  blocking collectives  32.3 us (8%)
  between operations  18 us (4%)
  matrix products  15.5 us (4%)
  starting transfers between devices  7.28 us (2%)
    unnamed x2, waiting for transfers between devices  192 us
    ppermute x32, waiting for transfers between devices, from_behind(): return lax.ppermute(block, axis, route)  60.6 us
    another operation x1, loops' own time, on_device(): final_carry = lax.fori_loop(0, lax.axis_size('dp'), travel, start_carry)  46.2 us
    psum x1, blocking collectives, on_device(): group_loss = lax.psum(loss_local, 'dp') / group_size  32.3 us
    reduce_sum x17, other arithmetic, unit_of(): jnp.sum(text_f32 * text_f32, axis=-1, keepdims=True) + 1e-06  11.2 us
    mul x16, other arithmetic, pair_terms(): image_grad = temp_scale * jnp.dot(logit_grad, unit_text, precision=highest)  10.4 us
    mul x16, other arithmetic, pair_terms(): unit_grad = temp_scale * jnp.dot(logit_grad.T, image_emb, precision=highest)  10.4 us
    dot_general x16, other arithmetic, pair_terms(): jnp.dot(image_emb, unit_text.T, precision=highest)  9.63 us
  transfers between devices with their start and end apart: 33, of which 17 were waited for; matrix products, arithmetic and copies ran while one was open for 10% of the time, Pallas kernels for 0%

commit v1 on v0

v1 whole, which is shorter than its diff:
```python
import jax
import jax.numpy as jnp
import numpy as np
from jax import lax
from jax.experimental import pallas as pl
from jax.experimental.pallas import tpu as pltpu
from jax.sharding import PartitionSpec as P

F32 = jnp.float32
BF16 = jnp.bfloat16
MESH = pl.DeviceIdType.MESH

ROWS, D, FF = 256, 1152, 4304
GROUP = 16
HALF = 2176
HALF1 = FF - HALF
K1 = 512
K_FULL, K_TAIL = FF // K1, FF % K1
CHUNK, HALF_CHUNK = 288, 144
SUB = 72
OWN = 9

ORDERS = (("y", "z", "x"), ("z", "x", "y"), ("x", "y", "z"))
BLOCKS = (
    (0, 0, 384),
    (1, 768, 384),
    (2, 1536, 384),
    (0, 384, 384),
    (1, 1152, 384),
    (2, 1920, 256),
)


def nt(a, b):
    return lax.dot_general(a, b, (((1,), (1,)), ((), ())), preferred_element_type=F32)


def tn(a, b):
    return lax.dot_general(a, b, (((0,), (0,)), ((), ())), preferred_element_type=F32)


def row_places():
    d = np.arange(D)
    digit = {"y": d // 288, "z": d // 72 % 4, "x": d // 18 % 4}
    rest = d % 18
    return np.stack(
        [
            digit[a] * 288 + digit[b] * 72 + digit[c] * 18 + rest
            for a, b, c in ORDERS[1:]
        ]
    ).astype(np.int32)


def kernel(
    hid_hbm,
    w_hbm,
    tok_hbm,
    gain_ref,
    text_ref,
    scale_ref,
    bias_ref,
    place_ref,
    loss_ref,
    gtext_ref,
    gtok_hbm,
    gw_ref,
    w_buf,
    hid,
    tok,
    resid,
    inv_buf,
    hcols,
    g_all,
    perm,
    g_t,
    texts,
    images,
    in_sems,
    w_sems,
    out_sem,
    x_send,
    x_recv,
    t_send,
    t_recv,
    i_send,
    i_recv,
    rs_send,
    rs_recv,
    *bufs,
):
    rep = lax.axis_index("replica")
    dp = lax.axis_index("dp")
    core = lax.rem(dp, 2)
    at = {
        "x": lax.rem(lax.div(dp, 2), 4),
        "y": lax.div(rep, 2),
        "z": lax.rem(rep, 2) * 2 + lax.div(dp, 8),
    }

    def device(where, which_core):
        return (
            where["y"] * 2 + lax.div(where["z"], 2),
            lax.rem(where["z"], 2) * 8 + where["x"] * 2 + which_core,
        )

    def moved(axis, distance):
        return {**at, axis: lax.rem(at[axis] + distance, 4)}

    partner = (rep, dp + 1 - 2 * core)

    def mate(distance):
        return (rep, lax.rem(dp + distance, GROUP))

    get_hid = pltpu.make_async_copy(hid_hbm, hid, in_sems.at[0])
    get_hid.start()

    def get_w(k, size=K1):
        rows = pl.ds(pl.multiple_of(k * K1, K1), size)
        return pltpu.make_async_copy(w_hbm.at[rows], w_buf.at[rows], w_sems.at[k])

    for k in range(K_FULL):
        get_w(k).start()
    get_w(K_FULL, K_TAIL).start()
    get_tok = pltpu.make_async_copy(tok_hbm, tok, in_sems.at[1])
    get_tok.start()
    my_first = pl.multiple_of(core * HALF, 128)
    get_cols = pltpu.make_async_copy(
        hid_hbm.at[pl.ds(my_first, HALF1)],
        hcols.at[pl.ds(0, HALF1), pl.ds(0, ROWS)],
        in_sems.at[2],
    )
    get_cols.start()
    get_more = pltpu.make_async_copy(
        hid_hbm.at[pl.ds(HALF1, HALF - HALF1)],
        hcols.at[pl.ds(HALF1, HALF - HALF1), pl.ds(0, ROWS)],
        in_sems.at[3],
    )

    @pl.when(core == 0)
    def _():
        get_more.start()

    barrier = pltpu.get_barrier_semaphore()
    peers = [mate(k) for k in range(1, GROUP)]
    peers += [device(moved("y", k), c) for k in (1, 2, 3) for c in (0, 1)]
    other = 2 - 2 * lax.rem(rep, 2)
    peers += [device({**at, "z": other + k}, c) for k in (0, 1) for c in (0, 1)]
    for peer in peers:
        pl.semaphore_signal(barrier, inc=1, device_id=peer, device_id_type=MESH)

    @pl.when(core == 1)
    def _():
        hcols[HALF1:, :] = jnp.zeros((HALF - HALF1, 2 * ROWS), BF16)

    texts[dp] = text_ref[...].astype(F32)
    for k in range(2):
        place = place_ref[pl.ds(k, 1), :]

        def fill(step, _, k=k, place=place):
            first = pl.multiple_of(step * 96, 96)
            rows = lax.broadcasted_iota(jnp.int32, (96, D), 0) + first
            hot = jnp.where(rows == place, 1.0, 0.0).astype(BF16)
            perm[k, pl.ds(first, 96), :] = hot
            return 0

        lax.fori_loop(0, D // 96, fill, 0)

    get_hid.wait()
    resid[...] = jnp.zeros((ROWS, D), F32)

    def product(k, _):
        get_w(k).wait()
        rows = pl.ds(pl.multiple_of(k * K1, K1), K1)
        resid[...] += tn(hid[rows, :], w_buf[rows, :])
        return 0

    lax.fori_loop(0, K_FULL, product, 0)
    get_w(K_FULL, K_TAIL).wait()
    resid[...] += tn(hid[K_FULL * K1 :, :], w_buf[K_FULL * K1 :, :])
    get_tok.wait()

    pl.semaphore_wait(barrier, len(peers))

    def spread(buf, send, recv, k):
        return pltpu.make_async_remote_copy(
            src_ref=buf.at[dp],
            dst_ref=buf.at[dp],
            send_sem=send.at[k - 1],
            recv_sem=recv.at[k - 1],
            device_id=mate(k),
            device_id_type=MESH,
        )

    for k in range(1, GROUP):
        spread(texts, t_send, t_recv, k).start()
    their_first = pl.multiple_of((1 - core) * HALF, 128)
    swap_cols = pltpu.make_async_remote_copy(
        src_ref=hid.at[pl.ds(their_first, HALF1)],
        dst_ref=hcols.at[pl.ds(0, HALF1), pl.ds(ROWS, ROWS)],
        send_sem=x_send.at[0],
        recv_sem=x_recv.at[0],
        device_id=partner,
        device_id_type=MESH,
    )
    swap_cols.start()
    swap_more = pltpu.make_async_remote_copy(
        src_ref=hid.at[pl.ds(HALF1, HALF - HALF1)],
        dst_ref=hcols.at[pl.ds(HALF1, HALF - HALF1), pl.ds(ROWS, ROWS)],
        send_sem=x_send.at[1],
        recv_sem=x_recv.at[1],
        device_id=partner,
        device_id_type=MESH,
    )

    @pl.when(core == 1)
    def _():
        swap_more.start()

    gain = gain_ref[...]
    step_rows = 32

    def norm(step, total):
        rows = pl.ds(pl.multiple_of(step * step_rows, step_rows), step_rows)
        value = resid[rows, :] + tok[rows, :].astype(F32)
        centred = value - jnp.mean(value, axis=-1, keepdims=True)
        var = jnp.mean(centred * centred, axis=-1, keepdims=True)
        inv = 1.0 / jnp.sqrt(var + 1e-06)
        unit = centred * inv
        resid[rows, :] = unit
        inv_buf[rows, :] = jnp.broadcast_to(inv, (step_rows, 128))
        return total + jnp.sum(unit, axis=0, keepdims=True)

    total = lax.fori_loop(0, ROWS // step_rows, norm, jnp.zeros((1, D), F32))
    pooled = total * gain * (1.0 / ROWS)
    pool_norm = jnp.sqrt(jnp.sum(pooled * pooled, axis=-1, keepdims=True) + 1e-06)
    image = pooled / pool_norm
    images[dp] = image
    for k in range(1, GROUP):
        spread(images, i_send, i_recv, k).start()

    scale = scale_ref[0]
    bias = bias_ref[0]
    for k in range(1, GROUP):
        spread(texts, t_send, t_recv, k).wait_recv()
    text_rows = texts[...].reshape(GROUP, D)
    text_norm = jnp.sqrt(jnp.sum(text_rows * text_rows, axis=-1, keepdims=True) + 1e-06)
    unit_text = text_rows / text_norm
    logits = scale * jnp.sum(unit_text * image, axis=-1, keepdims=True) + bias
    is_own = lax.broadcasted_iota(jnp.int32, (GROUP, 1), 0) == dp
    sign = jnp.where(is_own, 1.0, -1.0)
    dlogit = -sign * jax.nn.sigmoid(-sign * logits) / GROUP
    dimage = scale * jnp.sum(dlogit * unit_text, axis=0, keepdims=True)
    dpooled = (
        dimage - image * jnp.sum(image * dimage, axis=-1, keepdims=True)
    ) / pool_norm
    dxhat = dpooled * (1.0 / ROWS) * gain
    centre = dxhat - jnp.mean(dxhat, axis=-1, keepdims=True)

    def token_grad(step, _):
        rows = pl.ds(pl.multiple_of(step * step_rows, step_rows), step_rows)
        unit = resid[rows, :]
        along = jnp.mean(unit * dxhat, axis=-1, keepdims=True)
        grad = (centre - unit * along) * inv_buf[rows, :1]
        g_all[rows, :] = grad.astype(BF16)
        return 0

    lax.fori_loop(0, ROWS // step_rows, token_grad, 0)
    swap_grad = pltpu.make_async_remote_copy(
        src_ref=g_all.at[pl.ds(0, ROWS)],
        dst_ref=g_all.at[pl.ds(ROWS, ROWS)],
        send_sem=x_send.at[2],
        recv_sem=x_recv.at[2],
        device_id=partner,
        device_id_type=MESH,
    )
    swap_grad.start()
    put_grad = pltpu.make_async_copy(g_all.at[pl.ds(0, ROWS)], gtok_hbm, out_sem)
    put_grad.start()
    g_t[0, :, 0:ROWS] = g_all[0:ROWS, :].T

    get_cols.wait()
    swap_cols.wait_recv()

    @pl.when(core == 0)
    def _():
        get_more.wait()
        swap_more.wait_recv()

    swap_grad.wait_recv()
    g_t[0, :, ROWS:] = g_all[ROWS:, :].T

    def buffers(b):
        return bufs[11 * b : 11 * b + 11]

    def remote(b, k, src, dst, target):
        return pltpu.make_async_remote_copy(
            src_ref=src,
            dst_ref=dst,
            send_sem=rs_send.at[b, k],
            recv_sem=rs_recv.at[b, k],
            device_id=target,
            device_id_type=MESH,
        )

    top, low = pl.ds(0, HALF_CHUNK), pl.ds(HALF_CHUNK, HALF_CHUNK)

    def first_copy(b, k):
        far, to_right, to_left, relay, fr_left, fr_right = buffers(b)[:6]
        a = ORDERS[BLOCKS[b][0]][0]
        right, left = device(moved(a, 1), core), device(moved(a, 3), core)
        src, dst, target = (
            (far.at[top], relay.at[top], right),
            (far.at[low], relay.at[low], left),
            (to_right.at[low], fr_left.at[low], right),
            (to_left.at[top], fr_right.at[top], left),
            (to_right.at[top], fr_left.at[top], right),
            (to_left.at[low], fr_right.at[low], left),
        )[k]
        return remote(b, k, src, dst, target)

    def chunk(b, distance):
        part, first, width = BLOCKS[b]
        place = lax.rem(at[ORDERS[part][0]] + distance, 4)
        rows = pl.ds(pl.multiple_of(place * CHUNK, CHUNK), CHUNK)
        if part and b < 3:
            ordered = nt(perm[part - 1, rows, :], g_all[...])
            g_t[part, rows, :] = ordered.astype(BF16)
        return nt(g_t[part, rows, :], hcols[first : first + width, :])

    def far_chunk(b):
        far = buffers(b)[0]
        far[...] = chunk(b, 2).astype(BF16)
        first_copy(b, 0).start()
        first_copy(b, 1).start()

    def near_chunks(b):
        _, to_right, to_left = buffers(b)[:3]
        hold = buffers(b)[6]
        value = chunk(b, 1)
        to_right[HALF_CHUNK:, :] = value[HALF_CHUNK:, :].astype(BF16)
        first_copy(b, 2).start()
        hold[:HALF_CHUNK, :] = value[:HALF_CHUNK, :]
        value = chunk(b, 3)
        to_left[:HALF_CHUNK, :] = value[:HALF_CHUNK, :].astype(BF16)
        first_copy(b, 3).start()
        hold[HALF_CHUNK:, :] = value[HALF_CHUNK:, :]

    def pass_on(b):
        _, to_right, to_left, relay = buffers(b)[:4]
        hold = buffers(b)[6]
        first_copy(b, 0).wait_recv()
        to_right[:HALF_CHUNK, :] = (
            hold[:HALF_CHUNK, :] + relay[:HALF_CHUNK, :].astype(F32)
        ).astype(BF16)
        first_copy(b, 4).start()
        first_copy(b, 1).wait_recv()
        to_left[HALF_CHUNK:, :] = (
            hold[HALF_CHUNK:, :] + relay[HALF_CHUNK:, :].astype(F32)
        ).astype(BF16)
        first_copy(b, 5).start()

    def own_chunk(b):
        hold = buffers(b)[6]
        hold[...] = chunk(b, 0)

    def second_copies(b):
        send2, recv2 = buffers(b)[7:9]
        axis = ORDERS[BLOCKS[b][0]][1]
        return [
            remote(
                b,
                5 + k,
                send2.at[k - 1],
                recv2.at[k - 1],
                device(moved(axis, k), core),
            )
            for k in (1, 2, 3)
        ]

    def finish_first(b):
        fr_left, fr_right, hold, send2 = buffers(b)[4:8]
        axis = ORDERS[BLOCKS[b][0]][1]
        width = BLOCKS[b][2]
        for k in (2, 3, 4, 5):
            first_copy(b, k).wait_recv()
        hold[...] = hold[...] + fr_left[...].astype(F32) + fr_right[...].astype(F32)
        for k, copy in zip((1, 2, 3), second_copies(b)):
            place = lax.rem(at[axis] + k, 4)
            rows = pl.ds(pl.multiple_of(place * SUB, SUB), SUB)
            value = jnp.concatenate([hold[rows, :], jnp.zeros((8, width), F32)], axis=0)
            send2[k - 1] = value.astype(BF16)
            copy.start()

    def third_copies(b):
        send3, recv3 = buffers(b)[9:11]
        axis = ORDERS[BLOCKS[b][0]][2]
        mine = at[axis] * 2 + core
        out = []
        for k in range(1, 8):
            there = moved(axis, k // 2)
            its_core = core if k % 2 == 0 else 1 - core
            out.append(
                remote(
                    b,
                    8 + k,
                    send3.at[there[axis] * 2 + its_core],
                    recv3.at[mine],
                    device(there, its_core),
                )
            )
        return mine, out

    def finish_second(b):
        hold = buffers(b)[6]
        recv2, send3, recv3 = buffers(b)[8:11]
        axis = ORDERS[BLOCKS[b][0]][1]
        rows = pl.ds(pl.multiple_of(at[axis] * SUB, SUB), SUB)
        value = hold[rows, :]
        for k, copy in enumerate(second_copies(b)):
            copy.wait_recv()
            value = value + recv2[k].astype(F32)[:SUB, :]
        for k in range(8):
            send3[k] = value[k * OWN : (k + 1) * OWN, :]
        mine, copies = third_copies(b)
        for copy in copies:
            copy.start()
        recv3[mine] = send3[mine]

    def finish_third(b):
        recv3 = buffers(b)[10]
        _, first, width = BLOCKS[b]
        _, copies = third_copies(b)
        for copy in copies:
            copy.wait_recv()
        for half in (0, 1):
            value = (recv3[half] + recv3[2 + half]) + (recv3[4 + half] + recv3[6 + half])
            begin = half * HALF + first
            keep = min(width, FF - begin)
            gw_ref[:, begin : begin + keep] = value[:, :keep]

    early, late = (0, 1, 2), (3, 4, 5)
    for b in early:
        far_chunk(b)
    for b in early:
        near_chunks(b)
    for b in late:
        far_chunk(b)
    for b in early:
        pass_on(b)
    for b in late:
        near_chunks(b)
    for b in early:
        own_chunk(b)
    for b in late:
        pass_on(b)
    for b in late:
        own_chunk(b)

    for k in range(1, GROUP):
        spread(images, i_send, i_recv, k).wait_recv()
    image_rows = images[...].reshape(GROUP, D)
    all_logits = (
        scale
        * lax.dot_general(
            image_rows,
            unit_text,
            (((1,), (1,)), ((), ())),
            precision=lax.Precision.HIGHEST,
            preferred_element_type=F32,
        )
        + bias
    )
    row_id = lax.broadcasted_iota(jnp.int32, (GROUP, GROUP), 0)
    col_id = lax.broadcasted_iota(jnp.int32, (GROUP, GROUP), 1)
    signed = jnp.where(row_id == col_id, all_logits, -all_logits)
    soft = jnp.minimum(signed, 0.0) - jnp.log1p(jnp.exp(-jnp.abs(signed)))
    loss_ref[0] = -jnp.sum(soft) / GROUP
    own_text = texts[dp]
    own_norm = jnp.sqrt(jnp.sum(own_text * own_text, axis=-1, keepdims=True) + 1e-06)
    own_unit = own_text / own_norm
    column = scale * jnp.sum(image_rows * own_unit, axis=-1, keepdims=True) + bias
    dcolumn = -sign * jax.nn.sigmoid(-sign * column) / GROUP
    dunit = scale * jnp.sum(dcolumn * image_rows, axis=0, keepdims=True)
    gtext_ref[...] = (
        dunit - own_unit * jnp.sum(own_unit * dunit, axis=-1, keepdims=True)
    ) / own_norm

    for b in early:
        finish_first(b)
    for b in early:
        finish_second(b)
    for b in late:
        finish_first(b)
    for b in late:
        finish_second(b)
    for b in early + late:
        finish_third(b)

    put_grad.wait()
    for k in range(1, GROUP):
        spread(texts, t_send, t_recv, k).wait_send()
        spread(images, i_send, i_recv, k).wait_send()
    swap_cols.wait_send()
    swap_grad.wait_send()

    @pl.when(core == 1)
    def _():
        swap_more.wait_send()

    for b in early + late:
        for copy in (
            [first_copy(b, k) for k in range(6)] + second_copies(b) + third_copies(b)[1]
        ):
            copy.wait_send()


def block_scratch(width):
    return [
        pltpu.VMEM((CHUNK, width), BF16),
        pltpu.VMEM((CHUNK, width), BF16),
        pltpu.VMEM((CHUNK, width), BF16),
        pltpu.VMEM((CHUNK, width), BF16),
        pltpu.VMEM((CHUNK, width), BF16),
        pltpu.VMEM((CHUNK, width), BF16),
        pltpu.VMEM((CHUNK, width), F32),
        pltpu.VMEM((3, SUB + 8, width), BF16),
        pltpu.VMEM((3, SUB + 8, width), BF16),
        pltpu.VMEM((8, OWN, width), F32),
        pltpu.VMEM((8, OWN, width), F32),
    ]


def on_device(tokens, hidden, w_out, norm_gain, text_embed, logit_scale, logit_bias):
    vmem = pl.BlockSpec(memory_space=pltpu.VMEM)
    smem = pl.BlockSpec(memory_space=pltpu.SMEM)
    anywhere = pl.BlockSpec(memory_space=pl.ANY)
    dma = pltpu.SemaphoreType.DMA
    scratch = [
        pltpu.VMEM((FF, D), BF16),
        pltpu.VMEM((FF, ROWS), BF16),
        pltpu.VMEM((ROWS, D), BF16),
        pltpu.VMEM((ROWS, D), F32),
        pltpu.VMEM((ROWS, 128), F32),
        pltpu.VMEM((HALF, 2 * ROWS), BF16),
        pltpu.VMEM((2 * ROWS, D), BF16),
        pltpu.VMEM((2, D, D), BF16),
        pltpu.VMEM((3, D, 2 * ROWS), BF16),
        pltpu.VMEM((GROUP, 1, D), F32),
        pltpu.VMEM((GROUP, 1, D), F32),
        dma((4,)),
        dma((K_FULL + 1,)),
        dma,
        dma((3,)),
        dma((3,)),
        dma((GROUP - 1,)),
        dma((GROUP - 1,)),
        dma((GROUP - 1,)),
        dma((GROUP - 1,)),
        dma((len(BLOCKS), 16)),
        dma((len(BLOCKS), 16)),
    ]
    for _, _, width in BLOCKS:
        scratch += block_scratch(width)
    return pl.pallas_call(
        kernel,
        out_shape=(
            jax.ShapeDtypeStruct((1,), F32),
            jax.ShapeDtypeStruct((1, D), F32),
            jax.ShapeDtypeStruct((ROWS, D), BF16),
            jax.ShapeDtypeStruct((OWN, FF), F32),
        ),
        in_specs=[anywhere] * 3 + [vmem] * 2 + [smem] * 2 + [vmem],
        out_specs=(smem, vmem, anywhere, vmem),
        scratch_shapes=scratch,
        compiler_params=pltpu.CompilerParams(
            collective_id=0, has_side_effects=True, vmem_limit_bytes=60 * 2**20
        ),
    )(
        hidden.T,
        w_out.T,
        tokens,
        norm_gain.reshape(1, D),
        text_embed,
        logit_scale,
        logit_bias,
        jnp.asarray(row_places()),
    )


def solution(mesh):
    rows = P(("replica", "dp"), None)
    return jax.shard_map(
        on_device,
        mesh=mesh,
        in_specs=(rows, rows, P(), P(), rows, P(), P()),
        out_specs=(P("replica"), rows, rows, rows),
        check_vma=False,
    )
```

time: 425 us -> 68.4 us (0.16)
  waiting for transfers between devices: 253 us -> 0 us
  Pallas kernels: 0 us -> 58.1 us
  other arithmetic: 48.3 us -> 0 us
  loops' own time: 46.2 us -> 0 us
  blocking collectives: 32.3 us -> 0 us
  matrix products: 15.5 us -> 0 us
  between operations: 18 us -> 3.73 us
  starting transfers between devices: 7.28 us -> 0 us
    unnamed x2 -> x0, waiting for transfers between devices: 192 us -> none
    ppermute x32 -> x0, waiting for transfers between devices: 60.6 us -> none  [from_behind(): return lax.ppermute(block, axis, route)]
    pallas_call x0 -> x1, Pallas kernels: none -> 58.1 us  [on_device(): pl.pallas_call(kernel, out_shape=(jax.ShapeDtypeStruct((1,), F32), jax.Sh...]
    another operation x1 -> x0, loops' own time: 46.2 us -> none  [on_device(): final_carry = lax.fori_loop(0, lax.axis_size('dp'), travel, start_carry)]
    psum x1 -> x0, blocking collectives: 32.3 us -> none  [on_device(): group_loss = lax.psum(loss_local, 'dp') / group_size]
    mul x32 -> x0, other arithmetic: 20.8 us -> none  [the longest x16 10.4 us: pair_terms(): image_grad = temp_scale * jnp.dot(logit_grad, unit_text, precision=highest)]
    dot_general x2 -> x0, matrix products: 15.5 us -> none  [the longest x1 8.35 us: on_device(): lax.dot_general(tok_grad, hidden, (((0,), (0,)), ((), ())), preferred_ele...]
    reduce_sum x24 -> x0, other arithmetic: 15.1 us -> none  [the longest x17 11.2 us: unit_of(): jnp.sum(text_f32 * text_f32, axis=-1, keepdims=True) + 1e-06]
  transfers between devices with their start and end apart: 33 -> 0, of which waited for: 17 -> 0; matrix products, arithmetic and copies ran while one was open for 10% -> 0% of each run, Pallas kernels for 0% -> 0%
where the time goes in v1:
time: 68.4 us; the launch traced here: 68 us
  Pallas kernels  58.1 us (85%)
  local copies, waits for them, and re-layouts  6.18 us (9%)
  between operations  3.73 us (5%)
    pallas_call x1, Pallas kernels, on_device(): pl.pallas_call(kernel, out_shape=(jax.ShapeDtypeStruct((1,), F32), jax.Sh...  58.1 us
    unnamed x3, local copies, waits for them, and re-layouts  4.89 us

profile of v1, /device:TPU:1, one launch (start us, length us, event | category | flops | bytes accessed | tf_op | source)
XLA Modules:
  0.0 68.0 jit_solution(8534638812817133541)
XLA Ops:
  1.9 1.3 %reshape.11.gain_ref = f32[1,1152]{1,0:T(1,128)} reshape(f32[1152]{0:T(1024)} %param.11) | data formatting | bytes 9216 | tf_op jit(solution)/shard_map/reshape | solution.py:582
  3.2 58.1 %shard_map.111 = (f32[1]{0:T(128)}, f32[1,1152]{1,0:T(1,128)}, bf16[256,1152]{1,0:T(8,128)(2,1)}, f32[9,4304]{1,0:T(8,128)}) custom-call(bf16[4304,256]{1,0:T(8,128)(2,1)} %bitcast.3, bf16[4304,1152]{1,0:T(8,128)(2,1)} %bitcast.2, bf16[256,1152]{1,0:T(8,128)(2,1)} %tok_hbm.1, f32[1,1152]{1,0:T(1,128)} %reshape.11.gain_ref, bf16[1,1152]{1,0:T(2,128)(2,1)} %text_ref.1, ...), custom_call_target="tpu_custom_call" | custom-call | tf_op jit(solution)/shard_map/pallas_call | solution.py:564
  62.0 1.3 %copy.19 = f32[1,1152]{1,0:T(1,128)} copy(f32[1,1152]{1,0:T(1,128)} %get-tuple-element.9) | data formatting | bytes 9216
  63.3 1.9 %copy.20 = bf16[256,1152]{1,0:T(8,128)(2,1)} copy(bf16[256,1152]{1,0:T(8,128)(2,1)} %get-tuple-element.10) | data formatting | bytes 1179648
  65.2 1.7 %copy.21 = f32[9,4304]{1,0:T(8,128)} copy(f32[9,4304]{1,0:T(8,128)} %get-tuple-element.11) | data formatting | bytes 309888

commit v2 on v1

--- a/solution.py
+++ b/solution.py
@@ -14,7 +14,8 @@
 GROUP = 16
 HALF = 2176
 HALF1 = FF - HALF
-K1 = 512
+K1 = 1024
+BEFORE = 2
 K_FULL, K_TAIL = FF // K1, FF % K1
 CHUNK, HALF_CHUNK = 288, 144
 SUB = 72
@@ -28,6 +29,25 @@
     (0, 384, 384),
     (1, 1152, 384),
     (2, 1920, 256),
+)
+
+
+SCHEDULE = (
+    ("E", "far"),
+    ("E", "near"),
+    ("L", "far"),
+    ("E", "pass"),
+    ("L", "near"),
+    ("E", "own"),
+    ("L", "pass"),
+    ("L", "own"),
+    ("all", "loss"),
+    ("E", "first"),
+    ("L", "first"),
+    ("E", "second"),
+    ("L", "second"),
+    ("E", "third"),
+    ("L", "third"),
 )
 
 
@@ -55,15 +75,18 @@
     hid_hbm,
     w_hbm,
     tok_hbm,
-    gain_ref,
-    text_ref,
+    gain_hbm,
+    text_hbm,
     scale_ref,
     bias_ref,
-    place_ref,
+    place_hbm,
     loss_ref,
     gtext_ref,
     gtok_hbm,
     gw_ref,
+    gain_ref,
+    text_ref,
+    place_ref,
     w_buf,
     hid,
     tok,
@@ -111,6 +134,22 @@
     def mate(distance):
         return (rep, lax.rem(dp + distance, GROUP))
 
+    barrier = pltpu.get_barrier_semaphore()
+    peers = [mate(k) for k in range(1, GROUP)]
+    peers += [device(moved("y", k), c) for k in (1, 2, 3) for c in (0, 1)]
+    other = 2 - 2 * lax.rem(rep, 2)
+    peers += [device({**at, "z": other + k}, c) for k in (0, 1) for c in (0, 1)]
+    for peer in peers:
+        pl.semaphore_signal(barrier, inc=1, device_id=peer, device_id_type=MESH)
+
+    get_small = [
+        pltpu.make_async_copy(src, dst, in_sems.at[4 + k])
+        for k, (src, dst) in enumerate(
+            ((text_hbm, text_ref), (place_hbm, place_ref), (gain_hbm, gain_ref))
+        )
+    ]
+    for copy in get_small:
+        copy.start()
     get_hid = pltpu.make_async_copy(hid_hbm, hid, in_sems.at[0])
     get_hid.start()
 
@@ -140,18 +179,12 @@
     def _():
         get_more.start()
 
-    barrier = pltpu.get_barrier_semaphore()
-    peers = [mate(k) for k in range(1, GROUP)]
-    peers += [device(moved("y", k), c) for k in (1, 2, 3) for c in (0, 1)]
-    other = 2 - 2 * lax.rem(rep, 2)
-    peers += [device({**at, "z": other + k}, c) for k in (0, 1) for c in (0, 1)]
-    for peer in peers:
-        pl.semaphore_signal(barrier, inc=1, device_id=peer, device_id_type=MESH)
-
     @pl.when(core == 1)
     def _():
         hcols[HALF1:, :] = jnp.zeros((HALF - HALF1, 2 * ROWS), BF16)
 
+    for copy in get_small:
+        copy.wait()
     texts[dp] = text_ref[...].astype(F32)
     for k in range(2):
         place = place_ref[pl.ds(k, 1), :]
@@ -174,10 +207,7 @@
         resid[...] += tn(hid[rows, :], w_buf[rows, :])
         return 0
 
-    lax.fori_loop(0, K_FULL, product, 0)
-    get_w(K_FULL, K_TAIL).wait()
-    resid[...] += tn(hid[K_FULL * K1 :, :], w_buf[K_FULL * K1 :, :])
-    get_tok.wait()
+    lax.fori_loop(0, BEFORE, product, 0)
 
     pl.semaphore_wait(barrier, len(peers))
 
@@ -216,7 +246,12 @@
     def _():
         swap_more.start()
 
-    gain = gain_ref[...]
+    lax.fori_loop(BEFORE, K_FULL, product, 0)
+    get_w(K_FULL, K_TAIL).wait()
+    resid[...] += tn(hid[K_FULL * K1 :, :], w_buf[K_FULL * K1 :, :])
+    get_tok.wait()
+
+    gain = gain_ref[...].reshape(1, D)
     step_rows = 32
 
     def norm(step, total):
@@ -438,63 +473,51 @@
             keep = min(width, FF - begin)
             gw_ref[:, begin : begin + keep] = value[:, :keep]
 
-    early, late = (0, 1, 2), (3, 4, 5)
-    for b in early:
-        far_chunk(b)
-    for b in early:
-        near_chunks(b)
-    for b in late:
-        far_chunk(b)
-    for b in early:
-        pass_on(b)
-    for b in late:
-        near_chunks(b)
-    for b in early:
-        own_chunk(b)
-    for b in late:
-        pass_on(b)
-    for b in late:
-        own_chunk(b)
-
-    for k in range(1, GROUP):
-        spread(images, i_send, i_recv, k).wait_recv()
-    image_rows = images[...].reshape(GROUP, D)
-    all_logits = (
-        scale
-        * lax.dot_general(
-            image_rows,
-            unit_text,
-            (((1,), (1,)), ((), ())),
-            precision=lax.Precision.HIGHEST,
-            preferred_element_type=F32,
+    def group_terms():
+        for k in range(1, GROUP):
+            spread(images, i_send, i_recv, k).wait_recv()
+        image_rows = images[...].reshape(GROUP, D)
+        all_logits = (
+            scale
+            * lax.dot_general(
+                image_rows,
+                unit_text,
+                (((1,), (1,)), ((), ())),
+                precision=lax.Precision.HIGHEST,
+                preferred_element_type=F32,
+            )
+            + bias
         )
-        + bias
-    )
-    row_id = lax.broadcasted_iota(jnp.int32, (GROUP, GROUP), 0)
-    col_id = lax.broadcasted_iota(jnp.int32, (GROUP, GROUP), 1)
-    signed = jnp.where(row_id == col_id, all_logits, -all_logits)
-    soft = jnp.minimum(signed, 0.0) - jnp.log1p(jnp.exp(-jnp.abs(signed)))
-    loss_ref[0] = -jnp.sum(soft) / GROUP
-    own_text = texts[dp]
-    own_norm = jnp.sqrt(jnp.sum(own_text * own_text, axis=-1, keepdims=True) + 1e-06)
-    own_unit = own_text / own_norm
-    column = scale * jnp.sum(image_rows * own_unit, axis=-1, keepdims=True) + bias
-    dcolumn = -sign * jax.nn.sigmoid(-sign * column) / GROUP
-    dunit = scale * jnp.sum(dcolumn * image_rows, axis=0, keepdims=True)
-    gtext_ref[...] = (
-        dunit - own_unit * jnp.sum(own_unit * dunit, axis=-1, keepdims=True)
-    ) / own_norm
-
-    for b in early:
-        finish_first(b)
-    for b in early:
-        finish_second(b)
-    for b in late:
-        finish_first(b)
-    for b in late:
-        finish_second(b)
-    for b in early + late:
-        finish_third(b)
+        row_id = lax.broadcasted_iota(jnp.int32, (GROUP, GROUP), 0)
+        col_id = lax.broadcasted_iota(jnp.int32, (GROUP, GROUP), 1)
+        signed = jnp.where(row_id == col_id, all_logits, -all_logits)
+        soft = jnp.minimum(signed, 0.0) - jnp.log1p(jnp.exp(-jnp.abs(signed)))
+        loss_ref[0] = -jnp.sum(soft) / GROUP
+        own_text = texts[dp]
+        own_norm = jnp.sqrt(jnp.sum(own_text * own_text, axis=-1, keepdims=True) + 1e-06)
+        own_unit = own_text / own_norm
+        column = scale * jnp.sum(image_rows * own_unit, axis=-1, keepdims=True) + bias
+        dcolumn = -sign * jax.nn.sigmoid(-sign * column) / GROUP
+        dunit = scale * jnp.sum(dcolumn * image_rows, axis=0, keepdims=True)
+        gtext_ref[...] = (
+            dunit - own_unit * jnp.sum(own_unit * dunit, axis=-1, keepdims=True)
+        ) / own_norm
+
+    work = {
+        "far": far_chunk,
+        "near": near_chunks,
+        "pass": pass_on,
+        "own": own_chunk,
+        "first": finish_first,
+        "second": finish_second,
+        "third": finish_third,
+    }
+    for blocks, step in SCHEDULE:
+        if step == "loss":
+            group_terms()
+        else:
+            for b in (0, 1, 2) if blocks == "E" else (3, 4, 5):
+                work[step](b)
 
     put_grad.wait()
     for k in range(1, GROUP):
@@ -507,11 +530,18 @@
     def _():
         swap_more.wait_send()
 
-    for b in early + late:
+    for b in range(len(BLOCKS)):
         for copy in (
             [first_copy(b, k) for k in range(6)] + second_copies(b) + third_copies(b)[1]
         ):
             copy.wait_send()
+
+
+def hand_over(loss, gtext, gtok, gw, loss_out, gtext_out, gtok_out, gw_out):
+    loss_out[0] = loss[0]
+    gtext_out[...] = gtext[...]
+    gw_out[...] = gw[...]
+    gtok_out[...] = gtok[...]
 
 
 def block_scratch(width):
@@ -536,6 +566,9 @@
     anywhere = pl.BlockSpec(memory_space=pl.ANY)
     dma = pltpu.SemaphoreType.DMA
     scratch = [
+        pltpu.VMEM((D,), F32),
+        pltpu.VMEM((1, D), BF16),
+        pltpu.VMEM((2, D), jnp.int32),
         pltpu.VMEM((FF, D), BF16),
         pltpu.VMEM((FF, ROWS), BF16),
         pltpu.VMEM((ROWS, D), BF16),
@@ -547,7 +580,7 @@
         pltpu.VMEM((3, D, 2 * ROWS), BF16),
         pltpu.VMEM((GROUP, 1, D), F32),
         pltpu.VMEM((GROUP, 1, D), F32),
-        dma((4,)),
+        dma((7,)),
         dma((K_FULL + 1,)),
         dma,
         dma((3,)),
@@ -561,7 +594,7 @@
     ]
     for _, _, width in BLOCKS:
         scratch += block_scratch(width)
-    return pl.pallas_call(
+    made = pl.pallas_call(
         kernel,
         out_shape=(
             jax.ShapeDtypeStruct((1,), F32),
@@ -569,7 +602,7 @@
             jax.ShapeDtypeStruct((ROWS, D), BF16),
             jax.ShapeDtypeStruct((OWN, FF), F32),
         ),
-        in_specs=[anywhere] * 3 + [vmem] * 2 + [smem] * 2 + [vmem],
+        in_specs=[anywhere] * 5 + [smem] * 2 + [anywhere],
         out_specs=(smem, vmem, anywhere, vmem),
         scratch_shapes=scratch,
         compiler_params=pltpu.CompilerParams(
@@ -579,12 +612,18 @@
         hidden.T,
         w_out.T,
         tokens,
-        norm_gain.reshape(1, D),
+        norm_gain,
         text_embed,
         logit_scale,
         logit_bias,
         jnp.asarray(row_places()),
     )
+    return pl.pallas_call(
+        hand_over,
+        out_shape=tuple(jax.ShapeDtypeStruct(a.shape, a.dtype) for a in made),
+        in_specs=[smem, vmem, vmem, vmem],
+        out_specs=(smem, vmem, vmem, vmem),
+    )(*made)
 
 
 def solution(mesh):

time: 68.4 us -> 54.9 us (0.80)
  local copies, waits for them, and re-layouts: 6.18 us -> 0 us
  Pallas kernels: 58.1 us -> 52.8 us
  between operations: 3.73 us -> 1.93 us
    pallas_call x1, Pallas kernels: 58.1 us -> 50.1 us  [on_device(): pl.pallas_call(kernel, out_shape=(jax.ShapeDtypeStruct((1,), F32), jax.Sh...]
    unnamed x3 -> x0, local copies, waits for them, and re-layouts: 4.89 us -> none
    pallas_call x0 -> x1, Pallas kernels: none -> 2.78 us  [on_device(): pl.pallas_call(hand_over, out_shape=tuple((jax.ShapeDtypeStruct(a.shape,...]
    reshape x1 -> x0, local copies, waits for them, and re-layouts: 1.29 us -> none  [on_device(): norm_gain.reshape(1, D)]
where the time goes in v2:
time: 54.9 us; the launch traced here: 54.8 us
  Pallas kernels  52.8 us (96%)
  between operations  1.93 us (4%)
    pallas_call x1, Pallas kernels, on_device(): pl.pallas_call(kernel, out_shape=(jax.ShapeDtypeStruct((1,), F32), jax.Sh...  50.1 us
    pallas_call x1, Pallas kernels, on_device(): pl.pallas_call(hand_over, out_shape=tuple((jax.ShapeDtypeStruct(a.shape,...  2.78 us

profile of v2, /device:TPU:1, one launch (start us, length us, event | category | flops | bytes accessed | tf_op | source)
XLA Modules:
  0.0 54.8 jit_solution(1150031107546558974)
XLA Ops:
  1.9 50.1 %shard_map.111 = (f32[1]{0:T(128)}, f32[1,1152]{1,0:T(1,128)}, bf16[256,1152]{1,0:T(8,128)(2,1)}, f32[9,4304]{1,0:T(8,128)}) custom-call(bf16[4304,256]{1,0:T(8,128)(2,1)} %bitcast.3, bf16[4304,1152]{1,0:T(8,128)(2,1)} %bitcast.2, bf16[256,1152]{1,0:T(8,128)(2,1)} %tok_hbm.1, f32[1152]{0:T(1024)} %gain_hbm.1, bf16[1,1152]{1,0:T(2,128)(2,1)} %text_hbm.1, ...), custom_call_target="tpu_custom_call" | custom-call | tf_op jit(solution)/shard_map/pallas_call | solution.py:597
  52.0 2.8 %shard_map.112 = (f32[1]{0:T(128)}, f32[1,1152]{1,0:T(1,128)}, bf16[256,1152]{1,0:T(8,128)(2,1)}, f32[9,4304]{1,0:T(8,128)}) custom-call(f32[1]{0:T(128)} %get-tuple-element.8.loss, f32[1,1152]{1,0:T(1,128)} %get-tuple-element.9.gtext, bf16[256,1152]{1,0:T(8,128)(2,1)} %get-tuple-element.10.gtok, f32[9,4304]{1,0:T(8,128)} %get-tuple-element.11.gw), custom_call_target="tpu_custom_call" | custom-call | tf_op jit(solution)/shard_map/pallas_call | solution.py:621

commit v3 on v2

--- a/solution.py
+++ b/solution.py
@@ -1,6 +1,5 @@
 import jax
 import jax.numpy as jnp
-import numpy as np
 from jax import lax
 from jax.experimental import pallas as pl
 from jax.experimental.pallas import tpu as pltpu
@@ -15,39 +14,37 @@
 HALF = 2176
 HALF1 = FF - HALF
 K1 = 1024
-BEFORE = 2
+SWAPS = 4
+BEFORE = 0
 K_FULL, K_TAIL = FF // K1, FF % K1
 CHUNK, HALF_CHUNK = 288, 144
 SUB = 72
 OWN = 9
 
 ORDERS = (("y", "z", "x"), ("z", "x", "y"), ("x", "y", "z"))
-BLOCKS = (
-    (0, 0, 384),
-    (1, 768, 384),
-    (2, 1536, 384),
-    (0, 384, 384),
-    (1, 1152, 384),
-    (2, 1920, 256),
+TILES = ((3, 3, 3), (3, 3, 2))
+PART_AT = (0, 768, 1536)
+BLOCKS = tuple(
+    (p, PART_AT[p] + 128 * sum(t[p] for t in TILES[:g]), 128 * TILES[g][p])
+    for g in range(len(TILES))
+    for p in range(3)
 )
-
-
 SCHEDULE = (
-    ("E", "far"),
-    ("E", "near"),
-    ("L", "far"),
-    ("E", "pass"),
-    ("L", "near"),
-    ("E", "own"),
-    ("L", "pass"),
-    ("L", "own"),
-    ("all", "loss"),
-    ("E", "first"),
-    ("L", "first"),
-    ("E", "second"),
-    ("L", "second"),
-    ("E", "third"),
-    ("L", "third"),
+    (0, "far"),
+    (0, "near"),
+    (1, "far"),
+    (0, "pass"),
+    (1, "near"),
+    (0, "own"),
+    (1, "pass"),
+    (1, "own"),
+    (0, "loss"),
+    (0, "first"),
+    (1, "first"),
+    (0, "second"),
+    (1, "second"),
+    (0, "third"),
+    (1, "third"),
 )
 
 
@@ -59,16 +56,14 @@
     return lax.dot_general(a, b, (((0,), (0,)), ((), ())), preferred_element_type=F32)
 
 
-def row_places():
-    d = np.arange(D)
-    digit = {"y": d // 288, "z": d // 72 % 4, "x": d // 18 % 4}
-    rest = d % 18
-    return np.stack(
-        [
-            digit[a] * 288 + digit[b] * 72 + digit[c] * 18 + rest
-            for a, b, c in ORDERS[1:]
-        ]
-    ).astype(np.int32)
+def row_places(order):
+    rest = lax.broadcasted_iota(jnp.int32, (1, D), 1)
+    digit = {}
+    for axis, size in (("y", 288), ("z", 72), ("x", 18)):
+        count = sum(jnp.where(rest >= k * size, 1, 0) for k in (1, 2, 3))
+        rest = rest - count * size
+        digit[axis] = count
+    return sum(digit[axis] * size for axis, size in zip(order, (288, 72, 18))) + rest
 
 
 def kernel(
@@ -79,14 +74,12 @@
     text_hbm,
     scale_ref,
     bias_ref,
-    place_hbm,
     loss_ref,
     gtext_ref,
     gtok_hbm,
     gw_ref,
     gain_ref,
     text_ref,
-    place_ref,
     w_buf,
     hid,
     tok,
@@ -145,7 +138,7 @@
     get_small = [
         pltpu.make_async_copy(src, dst, in_sems.at[4 + k])
         for k, (src, dst) in enumerate(
-            ((text_hbm, text_ref), (place_hbm, place_ref), (gain_hbm, gain_ref))
+            ((text_hbm, text_ref), (gain_hbm, gain_ref))
         )
     ]
     for copy in get_small:
@@ -187,7 +180,7 @@
         copy.wait()
     texts[dp] = text_ref[...].astype(F32)
     for k in range(2):
-        place = place_ref[pl.ds(k, 1), :]
+        place = row_places(ORDERS[1 + k])
 
         def fill(step, _, k=k, place=place):
             first = pl.multiple_of(step * 96, 96)
@@ -299,16 +292,21 @@
         g_all[rows, :] = grad.astype(BF16)
         return 0
 
-    lax.fori_loop(0, ROWS // step_rows, token_grad, 0)
-    swap_grad = pltpu.make_async_remote_copy(
-        src_ref=g_all.at[pl.ds(0, ROWS)],
-        dst_ref=g_all.at[pl.ds(ROWS, ROWS)],
-        send_sem=x_send.at[2],
-        recv_sem=x_recv.at[2],
-        device_id=partner,
-        device_id_type=MESH,
-    )
-    swap_grad.start()
+    def swap_grad(k):
+        size = ROWS // SWAPS
+        return pltpu.make_async_remote_copy(
+            src_ref=g_all.at[pl.ds(k * size, size)],
+            dst_ref=g_all.at[pl.ds(ROWS + k * size, size)],
+            send_sem=x_send.at[2 + k],
+            recv_sem=x_recv.at[2 + k],
+            device_id=partner,
+            device_id_type=MESH,
+        )
+
+    steps = ROWS // step_rows // SWAPS
+    for k in range(SWAPS):
+        lax.fori_loop(k * steps, (k + 1) * steps, token_grad, 0)
+        swap_grad(k).start()
     put_grad = pltpu.make_async_copy(g_all.at[pl.ds(0, ROWS)], gtok_hbm, out_sem)
     put_grad.start()
     g_t[0, :, 0:ROWS] = g_all[0:ROWS, :].T
@@ -321,7 +319,8 @@
         get_more.wait()
         swap_more.wait_recv()
 
-    swap_grad.wait_recv()
+    for k in range(SWAPS):
+        swap_grad(k).wait_recv()
     g_t[0, :, ROWS:] = g_all[ROWS:, :].T
 
     def buffers(b):
@@ -512,11 +511,11 @@
         "second": finish_second,
         "third": finish_third,
     }
-    for blocks, step in SCHEDULE:
+    for group, step in SCHEDULE:
         if step == "loss":
             group_terms()
         else:
-            for b in (0, 1, 2) if blocks == "E" else (3, 4, 5):
+            for b in range(3 * group, 3 * group + 3):
                 work[step](b)
 
     put_grad.wait()
@@ -524,7 +523,8 @@
         spread(texts, t_send, t_recv, k).wait_send()
         spread(images, i_send, i_recv, k).wait_send()
     swap_cols.wait_send()
-    swap_grad.wait_send()
+    for k in range(SWAPS):
+        swap_grad(k).wait_send()
 
     @pl.when(core == 1)
     def _():
@@ -568,7 +568,6 @@
     scratch = [
         pltpu.VMEM((D,), F32),
         pltpu.VMEM((1, D), BF16),
-        pltpu.VMEM((2, D), jnp.int32),
         pltpu.VMEM((FF, D), BF16),
         pltpu.VMEM((FF, ROWS), BF16),
         pltpu.VMEM((ROWS, D), BF16),
@@ -583,8 +582,8 @@
         dma((7,)),
         dma((K_FULL + 1,)),
         dma,
-        dma((3,)),
-        dma((3,)),
+        dma((2 + SWAPS,)),
+        dma((2 + SWAPS,)),
         dma((GROUP - 1,)),
         dma((GROUP - 1,)),
         dma((GROUP - 1,)),
@@ -602,7 +601,7 @@
             jax.ShapeDtypeStruct((ROWS, D), BF16),
             jax.ShapeDtypeStruct((OWN, FF), F32),
         ),
-        in_specs=[anywhere] * 5 + [smem] * 2 + [anywhere],
+        in_specs=[anywhere] * 5 + [smem] * 2,
         out_specs=(smem, vmem, anywhere, vmem),
         scratch_shapes=scratch,
         compiler_params=pltpu.CompilerParams(
@@ -616,7 +615,6 @@
         text_embed,
         logit_scale,
         logit_bias,
-        jnp.asarray(row_places()),
     )
     return pl.pallas_call(
         hand_over,

time: 54.9 us -> 54.3 us (0.989)
  Pallas kernels: 52.8 us -> 52.2 us
    pallas_call x1, Pallas kernels: 50.1 us -> 49.4 us  [on_device(): pl.pallas_call(kernel, out_shape=(jax.ShapeDtypeStruct((1,), F32), jax.Sh...]
where the time goes in v3:
time: 54.3 us; the launch traced here: 54.1 us
  Pallas kernels  52.2 us (96%)
  between operations  1.93 us (4%)
    pallas_call x1, Pallas kernels, on_device(): pl.pallas_call(kernel, out_shape=(jax.ShapeDtypeStruct((1,), F32), jax.Sh...  49.4 us
    pallas_call x1, Pallas kernels, on_device(): pl.pallas_call(hand_over, out_shape=tuple((jax.ShapeDtypeStruct(a.shape,...  2.78 us

profile of v3, /device:TPU:1, one launch (start us, length us, event | category | flops | bytes accessed | tf_op | source)
XLA Modules:
  0.0 54.1 jit_solution(13463280207361921154)
XLA Ops:
  1.9 49.4 %shard_map.102 = (f32[1]{0:T(128)}, f32[1,1152]{1,0:T(1,128)}, bf16[256,1152]{1,0:T(8,128)(2,1)}, f32[9,4304]{1,0:T(8,128)}) custom-call(bf16[4304,256]{1,0:T(8,128)(2,1)} %bitcast.3, bf16[4304,1152]{1,0:T(8,128)(2,1)} %bitcast.2, bf16[256,1152]{1,0:T(8,128)(2,1)} %tok_hbm.1, f32[1152]{0:T(1024)} %gain_hbm.1, bf16[1,1152]{1,0:T(2,128)(2,1)} %text_hbm.1, ...), custom_call_target="tpu_custom_call" | custom-call | tf_op jit(solution)/shard_map/pallas_call | solution.py:596
  51.3 2.8 %shard_map.103 = (f32[1]{0:T(128)}, f32[1,1152]{1,0:T(1,128)}, bf16[256,1152]{1,0:T(8,128)(2,1)}, f32[9,4304]{1,0:T(8,128)}) custom-call(f32[1]{0:T(128)} %get-tuple-element.8.loss, f32[1,1152]{1,0:T(1,128)} %get-tuple-element.9.gtext, bf16[256,1152]{1,0:T(8,128)(2,1)} %get-tuple-element.10.gtok, f32[9,4304]{1,0:T(8,128)} %get-tuple-element.11.gw), custom_call_target="tpu_custom_call" | custom-call | tf_op jit(solution)/shard_map/pallas_call | solution.py:619

commit v4 on v3

--- a/solution.py
+++ b/solution.py
@@ -312,16 +312,10 @@
     g_t[0, :, 0:ROWS] = g_all[0:ROWS, :].T
 
     get_cols.wait()
-    swap_cols.wait_recv()
 
     @pl.when(core == 0)
     def _():
         get_more.wait()
-        swap_more.wait_recv()
-
-    for k in range(SWAPS):
-        swap_grad(k).wait_recv()
-    g_t[0, :, ROWS:] = g_all[ROWS:, :].T
 
     def buffers(b):
         return bufs[11 * b : 11 * b + 11]
@@ -361,9 +355,22 @@
             g_t[part, rows, :] = ordered.astype(BF16)
         return nt(g_t[part, rows, :], hcols[first : first + width, :])
 
+    def far_half(b, half):
+        part, first, width = BLOCKS[b]
+        place = lax.rem(at[ORDERS[part][0]] + 2, 4)
+        rows = pl.ds(pl.multiple_of(place * CHUNK, CHUNK), CHUNK)
+        held = pl.ds(half * ROWS, ROWS)
+        if part:
+            ordered = nt(perm[part - 1, rows, :], g_all[held, :])
+            g_t[part, rows, held] = ordered.astype(BF16)
+        return nt(g_t[part, rows, held], hcols[first : first + width, held])
+
     def far_chunk(b):
         far = buffers(b)[0]
-        far[...] = chunk(b, 2).astype(BF16)
+        if b < 3:
+            far[...] = (buffers(b)[6][...] + far_half(b, 1)).astype(BF16)
+        else:
+            far[...] = chunk(b, 2).astype(BF16)
         first_copy(b, 0).start()
         first_copy(b, 1).start()
 
@@ -511,6 +518,18 @@
         "second": finish_second,
         "third": finish_third,
     }
+    for b in range(3):
+        buffers(b)[6][...] = far_half(b, 0)
+    swap_cols.wait_recv()
+
+    @pl.when(core == 0)
+    def _():
+        swap_more.wait_recv()
+
+    for k in range(SWAPS):
+        swap_grad(k).wait_recv()
+    g_t[0, :, ROWS:] = g_all[ROWS:, :].T
+
     for group, step in SCHEDULE:
         if step == "loss":
             group_terms()

time: 54.3 us -> 55.1 us (1.015)
  Pallas kernels: 52.2 us -> 53 us
    pallas_call x1, Pallas kernels: 49.4 us -> 50.2 us  [on_device(): pl.pallas_call(kernel, out_shape=(jax.ShapeDtypeStruct((1,), F32), jax.Sh...]
where the time goes in v4:
time: 55.1 us; the launch traced here: 54.9 us
  Pallas kernels  53 us (96%)
  between operations  1.93 us (4%)
    pallas_call x1, Pallas kernels, on_device(): pl.pallas_call(kernel, out_shape=(jax.ShapeDtypeStruct((1,), F32), jax.Sh...  50.2 us
    pallas_call x1, Pallas kernels, on_device(): pl.pallas_call(hand_over, out_shape=tuple((jax.ShapeDtypeStruct(a.shape,...  2.78 us

profile of v4, /device:TPU:1, one launch (start us, length us, event | category | flops | bytes accessed | tf_op | source)
XLA Modules:
  0.0 54.9 jit_solution(7581072967196915543)
XLA Ops:
  1.9 50.2 %shard_map.102 = (f32[1]{0:T(128)}, f32[1,1152]{1,0:T(1,128)}, bf16[256,1152]{1,0:T(8,128)(2,1)}, f32[9,4304]{1,0:T(8,128)}) custom-call(bf16[4304,256]{1,0:T(8,128)(2,1)} %bitcast.3, bf16[4304,1152]{1,0:T(8,128)(2,1)} %bitcast.2, bf16[256,1152]{1,0:T(8,128)(2,1)} %tok_hbm.1, f32[1152]{0:T(1024)} %gain_hbm.1, bf16[1,1152]{1,0:T(2,128)(2,1)} %text_hbm.1, ...), custom_call_target="tpu_custom_call" | custom-call | tf_op jit(solution)/shard_map/pallas_call | solution.py:615
  52.1 2.8 %shard_map.103 = (f32[1]{0:T(128)}, f32[1,1152]{1,0:T(1,128)}, bf16[256,1152]{1,0:T(8,128)(2,1)}, f32[9,4304]{1,0:T(8,128)}) custom-call(f32[1]{0:T(128)} %get-tuple-element.8.loss, f32[1,1152]{1,0:T(1,128)} %get-tuple-element.9.gtext, bf16[256,1152]{1,0:T(8,128)(2,1)} %get-tuple-element.10.gtok, f32[9,4304]{1,0:T(8,128)} %get-tuple-element.11.gw), custom_call_target="tpu_custom_call" | custom-call | tf_op jit(solution)/shard_map/pallas_call | solution.py:638

commit v5 on v3

--- a/solution.py
+++ b/solution.py
@@ -263,8 +263,6 @@
     pool_norm = jnp.sqrt(jnp.sum(pooled * pooled, axis=-1, keepdims=True) + 1e-06)
     image = pooled / pool_norm
     images[dp] = image
-    for k in range(1, GROUP):
-        spread(images, i_send, i_recv, k).start()
 
     scale = scale_ref[0]
     bias = bias_ref[0]
@@ -309,6 +307,8 @@
         swap_grad(k).start()
     put_grad = pltpu.make_async_copy(g_all.at[pl.ds(0, ROWS)], gtok_hbm, out_sem)
     put_grad.start()
+    for k in range(1, GROUP):
+        spread(images, i_send, i_recv, k).start()
     g_t[0, :, 0:ROWS] = g_all[0:ROWS, :].T
 
     get_cols.wait()

time: 54.3 us -> 54.2 us (level)
  no operation moved by 1% of the time
where the time goes in v5:
time: 54.2 us; the launch traced here: 54 us
  Pallas kernels  52.1 us (96%)
  between operations  1.93 us (4%)
    pallas_call x1, Pallas kernels, on_device(): pl.pallas_call(kernel, out_shape=(jax.ShapeDtypeStruct((1,), F32), jax.Sh...  49.3 us
    pallas_call x1, Pallas kernels, on_device(): pl.pallas_call(hand_over, out_shape=tuple((jax.ShapeDtypeStruct(a.shape,...  2.78 us

profile of v5, /device:TPU:1, one launch (start us, length us, event | category | flops | bytes accessed | tf_op | source)
XLA Modules:
  0.0 54.0 jit_solution(8229864804110155725)
XLA Ops:
  1.9 49.3 %shard_map.102 = (f32[1]{0:T(128)}, f32[1,1152]{1,0:T(1,128)}, bf16[256,1152]{1,0:T(8,128)(2,1)}, f32[9,4304]{1,0:T(8,128)}) custom-call(bf16[4304,256]{1,0:T(8,128)(2,1)} %bitcast.3, bf16[4304,1152]{1,0:T(8,128)(2,1)} %bitcast.2, bf16[256,1152]{1,0:T(8,128)(2,1)} %tok_hbm.1, f32[1152]{0:T(1024)} %gain_hbm.1, bf16[1,1152]{1,0:T(2,128)(2,1)} %text_hbm.1, ...), custom_call_target="tpu_custom_call" | custom-call | tf_op jit(solution)/shard_map/pallas_call | solution.py:596
  51.2 2.8 %shard_map.103 = (f32[1]{0:T(128)}, f32[1,1152]{1,0:T(1,128)}, bf16[256,1152]{1,0:T(8,128)(2,1)}, f32[9,4304]{1,0:T(8,128)}) custom-call(f32[1]{0:T(128)} %get-tuple-element.8.loss, f32[1,1152]{1,0:T(1,128)} %get-tuple-element.9.gtext, bf16[256,1152]{1,0:T(8,128)(2,1)} %get-tuple-element.10.gtok, f32[9,4304]{1,0:T(8,128)} %get-tuple-element.11.gw), custom_call_target="tpu_custom_call" | custom-call | tf_op jit(solution)/shard_map/pallas_call | solution.py:619
